TPU v7x, 32 devices: a whole 2x2x4 slice. The times are simulated.
32 devices in a mesh: space: 8 (over z, core), vel: 4 (over y, x).
Axes of the slice: x: 2, y: 2, z: 4, core: 2. Of those that a mesh axis runs over, the one named last changes fastest.
Arguments:
- distribution: float32 [512, 32768], P('space', 'vel'), may hold values from 0.05 to 2
- collision_order: int32 [8, 64], P('space'), may hold values from 0 to 63, each once within a row
- collision_blocks: int32 [8], P('space'), may hold values from 1 to 4, 16 in all
- kernels: float32 [5, 32768], replicated, may hold values from -6 to 6
Outputs:
- new_distribution: float32 [512, 32768], P('space', 'vel')
Inputs may be any that keep to these rules, and one draw needn't show every extreme that they name: `collision_order`: each row is an ordering of the 64 local cells. `collision_blocks`: the counts sum to 16, which is 2 on average for each index of space, and the largest is 4.
All inputs are finite; a program needn't handle non-finite values. No bound on the sum of `collision_blocks` on one device may be relied on, other than what follows from the above.
Results may differ from a plain program's by a relative error of at most 0.0001.
Values sent between devices are 32-bit elements; how exact they have to be, the bound alone decides.
A program may use at most 128 MiB of HBM per device.

v0:
```python
import math

import jax
import jax.numpy as jnp
from jax import lax
from jax.sharding import PartitionSpec as P

NV = 32
QUAD = 2
BLOCK_CELLS = 16
KERN = 5


STEP_SCALE = 0.25
COURANT_MAX = 0.95
HIGHEST = lax.Precision.HIGHEST


def padded_2(cells, sides, width):
    for axis, dim in sides:
        count = lax.axis_size(axis)
        ends = count - 1
        head = lax.slice_in_dim(cells, 0, width, axis=dim)
        tail = lax.slice_in_dim(cells, cells.shape[dim] - width, cells.shape[dim], axis=dim)
        cells = jnp.concatenate(
            [
                lax.ppermute(tail, axis, [(i, (i + 1) % count) for i in range(ends)]),
                cells,
                lax.ppermute(head, axis, [((i + 1) % count, i) for i in range(ends)]),
            ],
            axis=dim,
        )
    return cells


def courants(vel_width):
    global_vel = lax.axis_index("vel") * vel_width + lax.iota(jnp.int32, vel_width)
    vx_plane = (global_vel // (NV * NV)).astype(jnp.float32)
    courant = COURANT_MAX * (2.0 * vx_plane - (NV - 1)) / (NV - 1)
    return (jnp.maximum(courant, 0.0), jnp.minimum(courant, 0.0))


def sweep(padded, upwind_pos, upwind_neg):
    centre = padded[1:-1]
    return centre - upwind_pos * (centre - padded[:-2]) - upwind_neg * (padded[2:] - centre)


def spectral_tables():
    line_index = lax.iota(jnp.int32, NV)
    phase_line = line_index[:, None] * line_index[None, :] % NV
    line_angle = phase_line.astype(jnp.float32) * (2.0 * math.pi / NV)
    cosine = jnp.cos(line_angle)
    sine = jnp.sin(line_angle)
    forward = jnp.stack([jnp.stack([cosine, sine]), jnp.stack([-sine, cosine])])
    backward = jnp.stack([jnp.stack([cosine, -sine]), jnp.stack([sine, cosine])])
    return (forward, backward)


def rotate_section(parts, table):
    pair_count, cell_total = (parts.shape[0], parts.shape[1])
    turned = jnp.einsum(
        "pqab,qcbm->pcma", table, parts, precision=HIGHEST, preferred_element_type=jnp.float32
    )
    return turned.reshape(table.shape[0], cell_total, NV, NV * NV)


def collide(cell_rows, kernels, tables):
    forward, backward = tables
    cell_total = cell_rows.shape[0]
    velocity_cube = cell_rows.reshape(cell_total, NV, NV * NV)
    spectrum = rotate_section(velocity_cube[None], forward[:, :1])
    spectrum = rotate_section(spectrum, forward)
    spectrum = rotate_section(spectrum, forward)
    weights = kernels.reshape(KERN, NV, NV * NV)

    def inverse(weight):
        mixed = rotate_section(spectrum * weight[None, None], backward)
        mixed = rotate_section(mixed, backward)
        mixed = rotate_section(mixed, backward[:1])
        return mixed[0] / NV**3

    gain_term = jnp.zeros_like(velocity_cube)
    for quad_index in range(QUAD):
        gain_term = gain_term + inverse(weights[2 * quad_index]) * inverse(
            weights[2 * quad_index + 1]
        )
    updated = velocity_cube + STEP_SCALE * (gain_term - velocity_cube * inverse(weights[2 * QUAD]))
    return updated.reshape(cell_total, NV**3)


def regroup(listed_rows, kernels, tables):
    vel_size = lax.axis_size("vel")
    row_total, vel_width = listed_rows.shape
    shaped = listed_rows.reshape(vel_size, row_total // vel_size, vel_width)
    result = collide(
        lax.all_to_all(shaped, "vel", split_axis=0, concat_axis=2, tiled=True)[0], kernels, tables
    )[None]
    result = lax.all_to_all(result, "vel", split_axis=2, concat_axis=0, tiled=True)
    return result.reshape(row_total, vel_width)


def local(distribution, collision_order, collision_blocks, kernels):
    cell_count, vel_width = distribution.shape
    upwind_pos, upwind_neg = courants(vel_width)
    padded = padded_2(distribution, (("space", 0),), 2)
    first_sweep = sweep(padded, upwind_pos, upwind_neg)
    position = lax.axis_index("space") * cell_count - 1 + lax.iota(jnp.int32, cell_count + 2)
    inside = (position >= 0) & (position < cell_count * lax.axis_size("space"))
    first_sweep = jnp.where(inside[:, None], first_sweep, 0.0)
    transported = sweep(first_sweep, upwind_pos, upwind_neg)
    tables = spectral_tables()
    cell_sequence = collision_order[0]
    rank_owned_blocks = collision_blocks[0]
    listed = transported[cell_sequence]
    collided = regroup(listed, kernels, tables)
    keep_rows = lax.iota(jnp.int32, cell_count) < BLOCK_CELLS * rank_owned_blocks
    updated = jnp.where(keep_rows[:, None], collided, listed)
    return transported.at[cell_sequence].set(updated)


def solution(mesh):
    return jax.shard_map(
        local,
        mesh=mesh,
        in_specs=(P("space", "vel"), P("space", None), P("space"), P()),
        out_specs=P("space", "vel"),
        check_vma=False,
    )
```

profile of v0, /device:TPU:0, one launch (start us, length us, event | category | flops | bytes accessed | tf_op | source)
XLA Modules:
  0.0 798.0 jit_solution(8882051118502463191)
XLA Ops:
  5.5 3.3 collective-permute-done.1
  8.8 3.8 fusion.27
  15.8 3.9 all-to-all-start
  19.7 5.1 slice_reduce_fusion
  25.2 19.7 %all-to-all-done = f32[4,16,8192]{2,1,0:T(8,128)S(1)} async-done(((f32[4,16,8192]{2,1,0:T(8,128)}), f32[4,16,8192]{2,1,0:T(8,128)S(1)}, u32[]{:S(2)}, u32[]{:S(2)}) %all-to-all-start) | async-done | bytes 2097184 | tf_op jit(solution)/shard_map/all_to_all | solution.py:96
  47.5 3.7 reshape.367
  51.2 7.1 convolution_bitcast_fusion
  58.3 10.5 %copy.107 = f32[2,16,1024,32]{3,2,0,1:T(8,128)} copy(f32[2,16,1024,32]{2,3,0,1:T(8,128)} %convolution_bitcast_fusion) | data formatting | bytes 8388608 | tf_op jit(solution)/shard_map/reshape | solution.py:64
  68.8 13.7 %reshape.369 = f32[2,16,32,1024,1]{3,2,0,1,4:T(8,128)} reshape(f32[2,16,1024,32]{3,2,0,1:T(8,128)} %copy.107) | data formatting | bytes 8388608 | tf_op jit(solution)/shard_map/reshape | solution.py:64
  82.5 7.2 fusion.29
  89.6 10.5 %copy.108 = f32[2,16,1024,32]{3,2,0,1:T(8,128)} copy(f32[2,16,1024,32]{2,3,0,1:T(8,128)} %fusion.29) | data formatting | bytes 8388608 | tf_op jit(solution)/shard_map/reshape | solution.py:64
  100.1 13.7 %reshape.372 = f32[2,16,32,1024,1]{3,2,0,1,4:T(8,128)} reshape(f32[2,16,1024,32]{3,2,0,1:T(8,128)} %copy.108) | data formatting | bytes 8388608 | tf_op jit(solution)/shard_map/reshape | solution.py:64
  113.8 7.4 fusion.32
  121.2 10.5 %copy.55 = f32[2,16,1024,32]{3,2,1,0:T(8,128)} copy(f32[2,16,1024,32]{2,3,0,1:T(8,128)} %fusion.32) | data formatting | bytes 8388608 | tf_op jit(solution)/shard_map/pqab,qcbm->pcma/transpose | solution.py:61
  131.7 13.7 %reshape.339 = f32[2,16,32,1024]{3,2,1,0:T(8,128)} reshape(f32[2,16,1024,32]{3,2,1,0:T(8,128)} %copy.55) | data formatting | bytes 8388608 | tf_op jit(solution)/shard_map/reshape | solution.py:64
  145.4 9.6 %multiply_bitcast_fusion = (f32[2,16,32,1024,1]{3,2,1,0,4:T(8,128)}, f32[2,16,32,1024,1]{3,2,1,0,4:T(8,128)}, f32[2,16,32,1024,1]{3,2,1,0,4:T(8,128)}, f32[2,16,...) fusion(f32[2,16,32,1024]{3,2,1,0:T(8,128)} %reshape.339, f32[32,1024]{1,0:T(8,128)S(1)} %mul.284, ...), kind=kLoop, calls=%fused_computation.26 | loop fusion | flops 5242880 | bytes 25821184 | tf_op jit(solution)/shard_map/mul | solution.py:77
  155.0 5.6 fusion.41
  160.6 10.5 %copy.114 = f32[2,16,1024,32]{3,2,0,1:T(8,128)} copy(f32[2,16,1024,32]{2,3,0,1:T(8,128)} %fusion.41) | data formatting | bytes 8388608 | tf_op jit(solution)/shard_map/reshape | solution.py:64
  171.1 13.7 %reshape.384 = f32[2,16,32,1024,1]{3,2,0,1,4:T(8,128)} reshape(f32[2,16,1024,32]{3,2,0,1:T(8,128)} %copy.114) | data formatting | bytes 8388608 | tf_op jit(solution)/shard_map/reshape | solution.py:64
  184.8 7.2 fusion.44
  191.9 10.5 %copy.63 = f32[2,16,1024,32]{3,2,1,0:T(8,128)} copy(f32[2,16,1024,32]{2,3,0,1:T(8,128)} %fusion.44) | data formatting | bytes 8388608 | tf_op jit(solution)/shard_map/pqab,qcbm->pcma/transpose | solution.py:61
  202.5 14.1 %reshape.343 = f32[2,16,32,1024]{3,2,1,0:T(8,128)} reshape(f32[2,16,1024,32]{3,2,1,0:T(8,128)} %copy.63) | data formatting | bytes 8388608 | tf_op jit(solution)/shard_map/reshape | solution.py:64
  216.5 4.5 fusion.92
  221.0 5.6 fusion.35
  226.6 10.5 %copy.111 = f32[2,16,1024,32]{3,2,0,1:T(8,128)} copy(f32[2,16,1024,32]{2,3,0,1:T(8,128)} %fusion.35) | data formatting | bytes 8388608 | tf_op jit(solution)/shard_map/reshape | solution.py:64
  237.1 13.7 %reshape.378 = f32[2,16,32,1024,1]{3,2,0,1,4:T(8,128)} reshape(f32[2,16,1024,32]{3,2,0,1:T(8,128)} %copy.111) | data formatting | bytes 8388608 | tf_op jit(solution)/shard_map/reshape | solution.py:64
  250.8 7.2 fusion.38
  257.9 10.5 %copy.59 = f32[2,16,1024,32]{3,2,1,0:T(8,128)} copy(f32[2,16,1024,32]{2,3,0,1:T(8,128)} %fusion.38) | data formatting | bytes 8388608 | tf_op jit(solution)/shard_map/pqab,qcbm->pcma/transpose | solution.py:61
  268.5 13.8 %reshape.341 = f32[2,16,32,1024]{3,2,1,0:T(8,128)} reshape(f32[2,16,1024,32]{3,2,1,0:T(8,128)} %copy.59) | data formatting | bytes 8388608 | tf_op jit(solution)/shard_map/reshape | solution.py:64
  282.3 6.2 fusion.94
  288.5 5.6 fusion.47
  294.1 10.5 %copy.117 = f32[2,16,1024,32]{3,2,0,1:T(8,128)} copy(f32[2,16,1024,32]{2,3,0,1:T(8,128)} %fusion.47) | data formatting | bytes 8388608 | tf_op jit(solution)/shard_map/reshape | solution.py:64
  304.6 13.7 %reshape.389 = f32[2,16,32,1024,1]{3,2,0,1,4:T(8,128)} reshape(f32[2,16,1024,32]{3,2,0,1:T(8,128)} %copy.117) | data formatting | bytes 8388608 | tf_op jit(solution)/shard_map/reshape | solution.py:64
  318.3 7.2 fusion.50
  325.5 10.5 %copy.67 = f32[2,16,1024,32]{3,2,1,0:T(8,128)} copy(f32[2,16,1024,32]{2,3,0,1:T(8,128)} %fusion.50) | data formatting | bytes 8388608 | tf_op jit(solution)/shard_map/pqab,qcbm->pcma/transpose | solution.py:61
  336.0 13.9 %reshape.345 = f32[2,16,32,1024]{3,2,1,0:T(8,128)} reshape(f32[2,16,1024,32]{3,2,1,0:T(8,128)} %copy.67) | data formatting | bytes 8388608 | tf_op jit(solution)/shard_map/reshape | solution.py:64
  349.9 6.2 fusion.90
  356.1 5.6 fusion.53
  361.7 10.5 %copy.120 = f32[2,16,1024,32]{3,2,0,1:T(8,128)} copy(f32[2,16,1024,32]{2,3,0,1:T(8,128)} %fusion.53) | data formatting | bytes 8388608 | tf_op jit(solution)/shard_map/reshape | solution.py:64
  372.2 13.7 %reshape.394 = f32[2,16,32,1024,1]{3,2,0,1,4:T(8,128)} reshape(f32[2,16,1024,32]{3,2,0,1:T(8,128)} %copy.120) | data formatting | bytes 8388608 | tf_op jit(solution)/shard_map/reshape | solution.py:64
  385.9 7.2 fusion.56
  393.1 10.5 %copy.71 = f32[2,16,1024,32]{3,2,1,0:T(8,128)} copy(f32[2,16,1024,32]{2,3,0,1:T(8,128)} %fusion.56) | data formatting | bytes 8388608 | tf_op jit(solution)/shard_map/pqab,qcbm->pcma/transpose | solution.py:61
  403.6 14.1 %reshape.347 = f32[2,16,32,1024]{3,2,1,0:T(8,128)} reshape(f32[2,16,1024,32]{3,2,1,0:T(8,128)} %copy.71) | data formatting | bytes 8388608 | tf_op jit(solution)/shard_map/reshape | solution.py:64
  417.7 7.9 fusion.70
  425.7 6.2 copy.72
  431.9 7.0 add.116
  438.9 7.2 fusion.59
  446.1 10.5 %copy.123 = f32[2,16,1024,32]{3,2,0,1:T(8,128)} copy(f32[2,16,1024,32]{2,3,0,1:T(8,128)} %fusion.59) | data formatting | bytes 8388608 | tf_op jit(solution)/shard_map/reshape | solution.py:64
  456.5 13.7 %reshape.399 = f32[2,16,32,1024,1]{3,2,0,1,4:T(8,128)} reshape(f32[2,16,1024,32]{3,2,0,1:T(8,128)} %copy.123) | data formatting | bytes 8388608 | tf_op jit(solution)/shard_map/reshape | solution.py:64
  470.2 7.2 fusion.62
  477.4 10.5 %copy.76 = f32[2,16,1024,32]{3,2,1,0:T(8,128)} copy(f32[2,16,1024,32]{2,3,0,1:T(8,128)} %fusion.62) | data formatting | bytes 8388608 | tf_op jit(solution)/shard_map/pqab,qcbm->pcma/transpose | solution.py:61
  487.9 13.8 %reshape.349 = f32[2,16,32,1024]{3,2,1,0:T(8,128)} reshape(f32[2,16,1024,32]{3,2,1,0:T(8,128)} %copy.76) | data formatting | bytes 8388608 | tf_op jit(solution)/shard_map/reshape | solution.py:64
  501.8 4.3 bitcast_multiply_fusion
  506.1 4.7 copy.77
  510.8 7.1 div.45
  520.4 24.0 %copy.78 = f32[1,16,32768]{1,0,2:T(1,128)} copy(f32[1,16,32768]{2,1,0:T(8,128)S(1)} %multiply_add_fusion) | data formatting | bytes 4194304 | tf_op jit(solution)/shard_map/add | solution.py:87
  544.9 146.5 %reduce.20 = f32[32768,16]{1,0:T(8,128)} reduce(f32[32768,1,16]{2,1,0:T(1,128)} %bitcast.240, f32[]{:T(128)} %broadcast.353), dimensions={1}, to_apply=%bitcast.232.reduce_sub_computation | reduce | bytes 4194308
  691.4 10.1 %reshape.444 = f32[4,1,131072]{2,1,0:T(1,128)} reshape(f32[32768,16]{1,0:T(8,128)} %reduce.20) | data formatting | bytes 4194304
  701.5 4.6 all-to-all-start.1
  706.8 25.4 %all-to-all-done.1 = f32[4,1,131072]{2,1,0:T(1,128)} async-done(((f32[4,1,131072]{2,1,0:T(1,128)}), f32[4,1,131072]{2,1,0:T(1,128)}, u32[]{:S(2)}, u32[]{:S(2)}) %all-to-all-start.1) | async-done | bytes 2097184 | tf_op jit(solution)/shard_map/all_to_all | solution.py:98
  732.3 7.7 reduce.21
  740.0 41.0 %reshape.445 = f32[32768,1,16]{2,1,0:T(1,128)} reshape(f32[4,131072]{1,0:T(4,128)S(1)} %reduce.21) | data formatting | bytes 4194304
  781.0 10.0 %copy.124 = f32[1,16,4,8192]{3,2,1,0:T(4,128)S(1)} copy(f32[1,16,4,8192]{1,3,2,0:T(8,128)} %bitcast.239) | data formatting | bytes 4194304 | tf_op jit(solution)/shard_map/all_to_all | solution.py:98
  793.3 4.6 scatter_fusion
  (47 shorter events, 16.9 us)
Async XLA Ops:
  1.1 4.4 collective-permute-start
  3.4 5.3 collective-permute-start.1
  5.5 3.3 copy-start.9
  13.3 2.5 copy-start
  15.8 29.1 %all-to-all-start = ((f32[4,16,8192]{2,1,0:T(8,128)}), f32[4,16,8192]{2,1,0:T(8,128)S(1)}, u32[]{:S(2)}, u32[]{:S(2)}) async-start(f32[4,16,8192]{2,1,0:T(8,128)} %bitcast.243), calls=%async_computation | async-start | bytes 4194304 | tf_op jit(solution)/shard_map/all_to_all | solution.py:96
  44.9 6.4 copy-start.1
  216.5 4.5 copy-start.6
  282.3 6.2 copy-start.5
  349.9 6.3 copy-start.4
  510.8 7.1 copy-start.2
  517.9 1.6 copy-start.7
  517.9 2.2 copy-start.8
  701.5 30.7 %all-to-all-start.1 = ((f32[4,1,131072]{2,1,0:T(1,128)}), f32[4,1,131072]{2,1,0:T(1,128)}, u32[]{:S(2)}, u32[]{:S(2)}) async-start(f32[4,1,131072]{2,1,0:T(1,128)} %reshape.444), calls=%async_computation.1 | async-start | bytes 4194304 | tf_op jit(solution)/shard_map/all_to_all | solution.py:98
  791.1 1.6 copy-start.3
  792.6 0.6 copy-start.10
where the time goes:
time: 806 us; the launch traced here: 798 us
  local copies, waits for them, and re-layouts  450 us (56%)
  other arithmetic  170 us (21%)
  matrix products  116 us (14%)
  waiting for transfers between devices  48.4 us (6%)
  starting transfers between devices  12.2 us (2%)
    reshape x20, local copies, waits for them, and re-layouts, rotate_section(): return turned.reshape(table.shape[0], cell_total, NV, NV * NV)  252 us
    unnamed x1, other arithmetic  146 us
    dot_general x18, matrix products, rotate_section(): jnp.einsum('pqab,qcbm->pcma', table, parts, precision=HIGHEST, preferred_...  116 us
    transpose x6, local copies, waits for them, and re-layouts, rotate_section(): jnp.einsum('pqab,qcbm->pcma', table, parts, precision=HIGHEST, preferred_...  63.2 us
    unnamed x25, local copies, waits for them, and re-layouts  54.5 us
    all_to_all x1, waiting for transfers between devices, regroup(): lax.all_to_all(result, 'vel', split_axis=2, concat_axis=0, tiled=True)  25.4 us
    add x1, local copies, waits for them, and re-layouts, collide(): velocity_cube + STEP_SCALE * (gain_term - velocity_cube * inverse(weights...  24 us
    all_to_all x1, waiting for transfers between devices, regroup(): lax.all_to_all(shaped, 'vel', split_axis=0, concat_axis=2, tiled=True)[0]  19.7 us
  transfers between devices with their start and end apart: 4, of which 3 were waited for; matrix products, arithmetic and copies ran while one was open for 1% of the time, Pallas kernels for 0%

commit v1 on v0

v1 whole, which is shorter than its diff:
```python
import functools
import math

import jax
import jax.numpy as jnp
import ml_dtypes
import numpy as np
from jax import lax
from jax.experimental import pallas as pl
from jax.experimental.pallas import tpu as pltpu
from jax.sharding import PartitionSpec as P

NV = 32
QUAD = 2
BLOCK_CELLS = 16
KERN = 5
STEP_SCALE = 0.25
COURANT_MAX = 0.95
LANES = 128
SUB = 8
GROUP = 4
MESH = pl.DeviceIdType.MESH
F32 = jnp.float32
BF16 = jnp.bfloat16


def split_np(matrix):
    high = matrix.astype(ml_dtypes.bfloat16)
    low = (matrix - high.astype(np.float64)).astype(ml_dtypes.bfloat16)
    return high, low


def left_form(matrix):
    real = np.block([[matrix.real, -matrix.imag], [matrix.imag, matrix.real]])
    high, low = split_np(real)
    return np.concatenate([high, low, high], axis=1)


def right_form(matrix):
    real = np.block([[matrix.real, matrix.imag], [-matrix.imag, matrix.real]])
    high, low = split_np(real)
    return np.concatenate([high, high, low], axis=0)


def dft_constants():
    turn = lambda phase: np.exp(-2j * math.pi * phase)
    r = np.repeat(np.arange(8), 16)[:, None]
    p = np.tile(np.arange(16), 8)[:, None]
    x0 = np.repeat(np.arange(16), 8)[None, :]
    y1 = np.tile(np.arange(8), 16)[None, :]
    y0 = np.repeat(np.arange(4), 32)[:, None]
    z = np.tile(np.arange(32), 4)[:, None]
    s, qz = y0.T, z.T
    rows = [turn(y1 * r / 8 + x0 * p / 16 + x0 * h / 32) for h in range(2)]
    lanes = turn(y0 * s / 4 + z * qz / 32)
    twist = turn(r * y0.T / 32)
    return (
        np.stack([left_form(m) for m in rows]),
        right_form(lanes),
        np.stack([left_form(m.conj().T) for m in rows]),
        right_form(lanes.conj().T),
        np.stack([twist.real, twist.imag]).astype(np.float32),
    )


def halves(value):
    high = value.astype(BF16)
    return high, (value - high.astype(F32)).astype(BF16)


def left_dot(table, value):
    high, low = halves(value)
    return jnp.dot(table, jnp.concatenate([high, high, low], axis=0), preferred_element_type=F32)


def right_dot(value, table):
    high, low = halves(value)
    return jnp.dot(jnp.concatenate([high, low, high], axis=1), table, preferred_element_type=F32)


def kernel(
    n_space, n_vel, cells, width,
    dist_ref, listed_ref, weight_ref, fr_ref, fl_ref, br_ref, bl_ref, tw_ref,
    out_ref,
    padded, halo_out, halo_in, sent, got, result, back, spectrum, parts,
    in_sem, halo_send, halo_recv, fs_sem, fr_sem, bs_sem, br_sem, own_sem,
):
    rows = width // LANES
    own = cells // n_vel
    groups = own // GROUP
    piece = GROUP * rows
    pairs = GROUP // 2
    me = lax.axis_index("vel")
    spot = lax.axis_index("space")
    right, left = lax.rem(spot + 1, n_space), lax.rem(spot + n_space - 1, n_space)

    load = pltpu.make_async_copy(dist_ref, padded.at[pl.ds(SUB, cells)], in_sem)
    load.start()
    barrier = pltpu.get_barrier_semaphore()
    for step in range(1, n_vel):
        pl.semaphore_signal(
            barrier, inc=1, device_id={"vel": lax.rem(me + step, n_vel)}, device_id_type=MESH
        )
    for side in (left, right):
        pl.semaphore_signal(barrier, inc=1, device_id={"space": side}, device_id_type=MESH)
    load.wait()

    @pl.loop(0, rows)
    def _(k):
        lanes = pl.ds(pl.multiple_of(k * LANES, LANES), LANES)
        halo_out[0, pl.ds(2 * k, 2), :] = padded[SUB:SUB + 2, lanes]
        halo_out[1, pl.ds(2 * k, 2), :] = padded[SUB + cells - 2:SUB + cells, lanes]

    pl.semaphore_wait(barrier, n_vel + 1)
    halo_copies = []
    for way, side in ((0, left), (1, right)):
        copy = pltpu.make_async_remote_copy(
            src_ref=halo_out.at[way],
            dst_ref=halo_in.at[1 - way],
            send_sem=halo_send.at[way],
            recv_sem=halo_recv.at[1 - way],
            device_id={"space": side},
            device_id_type=MESH,
        )
        copy.start()
        halo_copies.append(copy)
    for copy in halo_copies:
        copy.wait()

    total = cells + 2 * SUB
    position = lax.broadcasted_iota(jnp.int32, (total, LANES), 0) + (spot * cells - SUB)
    inside = (position >= 0) & (position < n_space * cells)

    @pl.loop(0, rows)
    def _(k):
        lanes = pl.ds(pl.multiple_of(k * LANES, LANES), LANES)
        padded[SUB - 2:SUB, lanes] = halo_in[0, pl.ds(2 * k, 2), :]
        padded[SUB + cells:SUB + cells + 2, lanes] = halo_in[1, pl.ds(2 * k, 2), :]
        plane = (me * rows + k) // SUB
        courant = COURANT_MAX * (2.0 * plane.astype(F32) - (NV - 1)) / (NV - 1)
        upwind_pos, upwind_neg = jnp.maximum(courant, 0.0), jnp.minimum(courant, 0.0)
        value = jnp.where(inside, padded[:, lanes], 0.0)
        for _ in range(2):
            before = pltpu.roll(value, 1, 0)
            after = pltpu.roll(value, total - 1, 0)
            value = value - upwind_pos * (value - before) - upwind_neg * (after - value)
            value = jnp.where(inside, value, 0.0)
        for tile in range(cells // SUB):
            sent[pl.ds(tile * SUB * rows + k, SUB, stride=rows), :] = value[
                (tile + 1) * SUB:(tile + 2) * SUB
            ]

    def forward(group, step):
        target = lax.rem(me + step, n_vel)
        return pltpu.make_async_remote_copy(
            src_ref=sent.at[pl.ds((target * groups + group) * piece, piece)],
            dst_ref=got.at[group, me],
            send_sem=fs_sem.at[group, step],
            recv_sem=fr_sem.at[group, step],
            device_id={"vel": target},
            device_id_type=MESH,
        )

    def backward(group, step):
        target = lax.rem(me + step, n_vel)
        return pltpu.make_async_remote_copy(
            src_ref=result.at[group, target],
            dst_ref=back.at[pl.ds((me * groups + group) * piece, piece)],
            send_sem=bs_sem.at[group, step],
            recv_sem=br_sem.at[group, step],
            device_id={"vel": target},
            device_id_type=MESH,
        )

    def own_in(group):
        return pltpu.make_async_copy(
            sent.at[pl.ds((me * groups + group) * piece, piece)], got.at[group, me],
            own_sem.at[0, group],
        )

    def own_out(group):
        return pltpu.make_async_copy(
            result.at[group, me], back.at[pl.ds((me * groups + group) * piece, piece)],
            own_sem.at[1, group],
        )

    for group in range(groups):
        for step in range(1, n_vel):
            forward(group, step).start()
        own_in(group).start()

    half = NV * SUB // 2

    @pl.loop(0, groups)
    def _(group):
        for step in range(1, n_vel):
            forward(group, step).wait_recv()
        own_in(group).wait()

        def cell(j):
            return jnp.concatenate(
                [got[group, m, j * rows:(j + 1) * rows, :] for m in range(n_vel)], axis=0
            )

        def stacked(lower):
            cut = slice(0, half) if lower else slice(half, 2 * half)
            return jnp.concatenate(
                [
                    jnp.concatenate([cell(2 * i)[cut], cell(2 * i + 1)[cut]], axis=0)
                    for i in range(pairs)
                ],
                axis=1,
            )

        twist_re, twist_im = tw_ref[0], tw_ref[1]
        low, high = stacked(True), stacked(False)
        for h, mixed in enumerate((low + high, low - high)):
            turned = left_dot(fr_ref[h], mixed)
            for i in range(pairs):
                re = turned[:half, i * LANES:(i + 1) * LANES]
                im = turned[half:, i * LANES:(i + 1) * LANES]
                spectrum[(2 * i + h) * half:(2 * i + h + 1) * half, :] = jnp.concatenate(
                    [re * twist_re - im * twist_im, re * twist_im + im * twist_re], axis=1
                )
        spectrum[...] = right_dot(spectrum[...], fl_ref[...])

        for table in range(KERN):
            weight = weight_ref[table]
            weights = jnp.concatenate([weight] * pairs, axis=0)
            weights = jnp.concatenate([weights, weights], axis=1)
            lined = right_dot(spectrum[...] * weights, bl_ref[...])
            halves_out = []
            for h in range(2):
                columns = []
                for i in range(pairs):
                    block = lined[(2 * i + h) * half:(2 * i + h + 1) * half]
                    re, im = block[:, :LANES], block[:, LANES:]
                    columns.append(
                        jnp.concatenate(
                            [re * twist_re + im * twist_im, im * twist_re - re * twist_im], axis=0
                        )
                    )
                halves_out.append(left_dot(br_ref[h], jnp.concatenate(columns, axis=1)))
            even, odd = halves_out
            for place, value in ((0, even + odd), (1, even - odd)):
                if table == 0:
                    parts[place] = value
                elif table == 1:
                    parts[place] = parts[place] * value
                elif table == 2:
                    parts[2 + place] = value
                elif table == 3:
                    parts[place] = parts[place] + parts[2 + place] * value
                else:
                    parts[place] = parts[place] - stacked(place == 0) * value

        for j in range(GROUP):
            flag = listed_ref[pl.ds((me * groups + group) * GROUP + j, 1), :] > 0.0
            i, component = j // 2, j % 2
            for m in range(n_vel):
                place, start = (m * rows) // half, (m * rows) % half
                change = parts[
                    place,
                    component * half + start:component * half + start + rows,
                    i * LANES:(i + 1) * LANES,
                ]
                old = got[group, m, j * rows:(j + 1) * rows, :]
                result[group, m, j * rows:(j + 1) * rows, :] = jnp.where(
                    flag, old + STEP_SCALE * change, old
                )
        for step in range(1, n_vel):
            backward(group, step).start()
        own_out(group).start()

    for group in range(groups):
        for step in range(1, n_vel):
            forward(group, step).wait_send()
            backward(group, step).wait()
        own_out(group).wait()

    @pl.loop(0, rows)
    def _(k):
        lanes = pl.ds(pl.multiple_of(k * LANES, LANES), LANES)
        for tile in range(cells // SUB):
            out_ref[tile * SUB:(tile + 1) * SUB, lanes] = back[
                pl.ds(tile * SUB * rows + k, SUB, stride=rows), :
            ]


def packed_weights(kernels):
    cube = kernels.reshape(KERN, NV, NV, NV)
    mirrored = jnp.roll(jnp.flip(cube, (1, 2, 3)), (1, 1, 1), (1, 2, 3))
    even = (cube + mirrored) * (0.5 / NV**3)
    even = even.reshape(KERN, NV // 2, 2, 4, 8, NV).transpose(0, 2, 4, 1, 3, 5)
    return even.reshape(KERN, NV * SUB, LANES)


def local(n_space, n_vel, distribution, collision_order, collision_blocks, kernels):
    cells, width = distribution.shape
    rows = width // LANES
    own = cells // n_vel
    groups = own // GROUP
    piece = GROUP * rows
    slot = lax.iota(jnp.int32, cells)
    chosen = (slot < BLOCK_CELLS * collision_blocks[0])[:, None]
    hit = (collision_order[0][:, None] == slot[None, :]) & chosen
    listed = jnp.broadcast_to(jnp.max(hit.astype(F32), axis=0)[:, None], (cells, LANES))
    weights = packed_weights(kernels)
    constants = [jnp.asarray(c) for c in dft_constants()]
    vmem = pl.BlockSpec(memory_space=pltpu.VMEM)
    dma = pltpu.SemaphoreType.DMA
    return pl.pallas_call(
        functools.partial(kernel, n_space, n_vel, cells, width),
        out_shape=jax.ShapeDtypeStruct((cells, width), F32),
        in_specs=[pl.BlockSpec(memory_space=pl.ANY)] + [vmem] * 7,
        out_specs=vmem,
        scratch_shapes=[
            pltpu.VMEM((cells + 2 * SUB, width), F32),
            pltpu.VMEM((2, 2 * rows, LANES), F32),
            pltpu.VMEM((2, 2 * rows, LANES), F32),
            pltpu.VMEM((cells * rows, LANES), F32),
            pltpu.VMEM((groups, n_vel, piece, LANES), F32),
            pltpu.VMEM((groups, n_vel, piece, LANES), F32),
            pltpu.VMEM((cells * rows, LANES), F32),
            pltpu.VMEM((GROUP // 2 * NV * SUB, 2 * LANES), F32),
            pltpu.VMEM((4, NV * SUB, GROUP // 2 * LANES), F32),
            dma,
            dma((2,)),
            dma((2,)),
            dma((groups, n_vel)),
            dma((groups, n_vel)),
            dma((groups, n_vel)),
            dma((groups, n_vel)),
            dma((2, groups)),
        ],
        compiler_params=pltpu.CompilerParams(
            collective_id=0, has_side_effects=True, vmem_limit_bytes=48 * 2**20
        ),
    )(distribution, listed, weights, *constants)


def solution(mesh):
    return jax.shard_map(
        functools.partial(local, mesh.shape["space"], mesh.shape["vel"]),
        mesh=mesh,
        in_specs=(P("space", "vel"), P("space", None), P("space"), P()),
        out_specs=P("space", "vel"),
        check_vma=False,
    )
```

time: 806 us -> 90.6 us (0.11)
  local copies, waits for them, and re-layouts: 450 us -> 21.6 us
  other arithmetic: 170 us -> 5.98 us
  matrix products: 116 us -> 0 us
  Pallas kernels: 0 us -> 61.9 us
  waiting for transfers between devices: 48.4 us -> 0 us
  starting transfers between devices: 12.2 us -> 0 us
    reshape x20 -> x3, local copies, waits for them, and re-layouts: 252 us -> 8.4 us  [the longest x2 5.62 us: packed_weights(): cube = kernels.reshape(KERN, NV, NV, NV)]
    unnamed x1 -> x0, other arithmetic: 146 us -> none
    dot_general x18 -> x0, matrix products: 116 us -> none  [rotate_section(): jnp.einsum('pqab,qcbm->pcma', table, parts, precision=HIGHEST, preferred_...]
    pallas_call x0 -> x1, Pallas kernels: none -> 61.9 us  [local(): pl.pallas_call(functools.partial(kernel, n_space, n_vel, cells, width), o...]
    transpose x6 -> x1, local copies, waits for them, and re-layouts: 63.2 us -> 2.24 us  [packed_weights(): even = even.reshape(KERN, NV // 2, 2, 4, 8, NV).transpose(0, 2, 4, 1, 3, 5)]
    unnamed x25 -> x13, local copies, waits for them, and re-layouts: 54.5 us -> 1.35 us
    all_to_all x2 -> x0, waiting for transfers between devices: 45.1 us -> none  [the longest x1 25.4 us: regroup(): lax.all_to_all(result, 'vel', split_axis=2, concat_axis=0, tiled=True)]
    add x3 -> x0, local copies, waits for them, and re-layouts: 37.2 us -> none  [the longest x1 24 us: collide(): velocity_cube + STEP_SCALE * (gain_term - velocity_cube * inverse(weights...]
  transfers between devices with their start and end apart: 4 -> 0, of which waited for: 3 -> 0; matrix products, arithmetic and copies ran while one was open for 1% -> 0% of each run, Pallas kernels for 0% -> 0%
where the time goes in v1:
time: 90.6 us; the launch traced here: 90.2 us
  Pallas kernels  61.9 us (68%)
  local copies, waits for them, and re-layouts  21.6 us (24%)
  other arithmetic  5.98 us (7%)
    pallas_call x1, Pallas kernels, local(): pl.pallas_call(functools.partial(kernel, n_space, n_vel, cells, width), o...  61.9 us
    slice x5, local copies, waits for them, and re-layouts, packed_weights(): mirrored = jnp.roll(jnp.flip(cube, (1, 2, 3)), (1, 1, 1), (1, 2, 3))  9.49 us
    reshape x2, local copies, waits for them, and re-layouts, packed_weights(): cube = kernels.reshape(KERN, NV, NV, NV)  5.62 us
    transpose x1, other arithmetic, packed_weights(): even = even.reshape(KERN, NV // 2, 2, 4, 8, NV).transpose(0, 2, 4, 1, 3, 5)  3.44 us
    reshape x1, local copies, waits for them, and re-layouts, packed_weights(): return even.reshape(KERN, NV * SUB, LANES)  2.78 us
    concatenate x1, other arithmetic, packed_weights(): mirrored = jnp.roll(jnp.flip(cube, (1, 2, 3)), (1, 1, 1), (1, 2, 3))  2.44 us
    transpose x1, local copies, waits for them, and re-layouts, packed_weights(): even = even.reshape(KERN, NV // 2, 2, 4, 8, NV).transpose(0, 2, 4, 1, 3, 5)  2.24 us

profile of v1, /device:TPU:0, one launch (start us, length us, event | category | flops | bytes accessed | tf_op | source)
XLA Modules:
  0.0 90.2 jit_solution(9794863161664104155)
XLA Ops:
  0.0 2.1 %reshape.21 = f32[5,32,32,32]{3,2,1,0:T(8,128)S(1)} reshape(f32[5,32768]{1,0:T(8,128)} %param.12) | data formatting | bytes 1310720 | tf_op jit(solution)/shard_map/reshape | solution.py:291
  2.1 1.8 %slice.39 = f32[5,31,32,32]{3,2,1,0:T(8,128)} slice(f32[5,32,32,32]{3,2,1,0:T(8,128)S(1)} %reshape.21), slice={[0:5], [1:32], [0:32], [0:32]} | slice | bytes 1269760 | tf_op jit(solution)/shard_map/jit(_roll_static)/slice | solution.py:292
  3.9 5.3 %slice.33 = f32[5,31,32,32]{3,2,1,0:T(8,128)} reverse(f32[5,31,32,32]{3,2,1,0:T(8,128)} %slice.39), dimensions={1,2,3} | reverse | bytes 1269760 | tf_op jit(solution)/shard_map/jit(_roll_static)/slice | solution.py:292
  9.2 0.1 slice.31
  9.3 2.4 %fusion = f32[5,32,32,32]{3,2,1,0:T(8,128)S(1)} fusion(f32[5,31,32,32]{3,2,1,0:T(8,128)} %slice.33, f32[5,1,32,32]{3,2,1,0:T(8,128)S(1)} %slice.31), kind=kLoop, calls=%fused_computation.1 | loop fusion | flops 491520 | bytes 1310720 | tf_op jit(solution)/shard_map/jit(_roll_static)/concatenate | solution.py:292
  11.8 2.3 %slice.40 = f32[5,32,32,1]{3,2,1,0:T(8,128)} slice(f32[5,32,32,32]{3,2,1,0:T(8,128)S(1)} %fusion), slice={[0:5], [0:32], [0:32], [31:32]} | slice | bytes 40960 | tf_op jit(solution)/shard_map/jit(_roll_static)/slice | solution.py:292
  14.0 3.6 %reshape.20 = f32[5,16,2,4,8,32]{5,4,3,2,1,0:T(8,128)} reshape(f32[5,32768]{1,0:T(8,128)} %param.12) | data formatting | bytes 1310720 | tf_op jit(solution)/shard_map/reshape | solution.py:291
  17.6 3.4 %fusion.2 = f32[5,2,8,16,4,32]{5,2,4,1,3,0:T(8,128)S(1)} fusion(f32[5,16,2,4,8,32]{5,4,3,2,1,0:T(8,128)} %reshape.20, f32[5,16,2,4,8,31]{5,4,3,2,1,0:T(8,128)S(1)} %bitcast.7, f32[5,16,2,4,8,1]{5,4,3,2,1,0:T(8,128)} %bitcast.8), kind=kLoop, calls=%fused_computation.5 | loop fusion | flops 491520 | bytes 1966080 | tf_op jit(solution)/shard_map/transpose | solution.py:294
  21.0 2.2 %copy.14 = f32[5,2,8,16,4,32]{5,4,3,2,1,0:T(4,128)} copy(f32[5,2,8,16,4,32]{5,2,4,1,3,0:T(8,128)S(1)} %fusion.2) | data formatting | bytes 1310720 | tf_op jit(solution)/shard_map/transpose | solution.py:294
  23.3 0.0 copy-start.5
  23.3 0.0 copy-start
  23.3 0.0 copy-start.1
  23.3 0.0 copy-start.2
  23.3 0.0 copy-start.3
  23.3 0.0 copy-start.4
  23.3 2.8 %reshape.22.weight_ref = f32[5,256,128]{2,1,0:T(8,128)S(1)} reshape(f32[5,2,8,16,4,32]{5,4,3,2,1,0:T(4,128)} %copy.14) | data formatting | bytes 1310720 | tf_op jit(solution)/shard_map/reshape | solution.py:295
  26.7 0.0 copy-done.5
  26.8 0.1 convert_reduce_fusion
  26.9 0.1 broadcast_in_dim.2.listed_ref
  26.9 0.0 copy-done
  26.9 0.0 copy-done.1
  26.9 0.0 copy-done.2
  26.9 0.0 copy-done.3
  27.0 0.0 copy-done.4
  27.0 61.9 %shard_map.91 = f32[64,8192]{1,0:T(8,128)S(1)} custom-call(f32[64,8192]{1,0:T(8,128)} %dist_ref.1, f32[64,128]{1,0:T(8,128)S(1)} %broadcast_in_dim.2.listed_ref, f32[5,256,128]{2,1,0:T(8,128)S(1)} %reshape.22.weight_ref, bf16[2,256,768]{2,1,0:T(8,128)(2,1)S(1)} %copy-done, bf16[768,256]{1,0:T(8,128)(2,1)S(1)} %copy-done.2, ...), custom_call_target="tpu_custom_call" | custom-call | tf_op jit(solution)/shard_map/pallas_call | solution.py:312
  88.9 1.3 %copy.17 = f32[64,8192]{1,0:T(8,128)} copy(f32[64,8192]{1,0:T(8,128)S(1)} %shard_map.91) | data formatting | bytes 4194304
  (2 shorter events, 0.0 us)
Async XLA Ops:
  23.3 3.5 %copy-start.5 = (s32[1,64]{1,0:T(1,128)S(1)}, s32[1,64]{1,0:T(1,128)}, u32[]{:S(2)}) copy-start(s32[1,64]{1,0:T(1,128)} %param.10) | copy-start | bytes 772
  23.3 3.7 %copy-start = (bf16[2,256,768]{2,1,0:T(8,128)(2,1)S(1)}, bf16[2,256,768]{2,1,0:T(8,128)(2,1)}, u32[]{:S(2)}) copy-start(bf16[2,256,768]{2,1,0:T(8,128)(2,1)} %constant.17.clone.fr_ref) | copy-start | bytes 2359300
  23.3 3.7 %copy-start.1 = (bf16[2,256,768]{2,1,0:T(8,128)(2,1)S(1)}, bf16[2,256,768]{2,1,0:T(8,128)(2,1)}, u32[]{:S(2)}) copy-start(bf16[2,256,768]{2,1,0:T(8,128)(2,1)} %constant.19.clone.br_ref) | copy-start | bytes 2359300
  23.3 3.7 %copy-start.2 = (bf16[768,256]{1,0:T(8,128)(2,1)S(1)}, bf16[768,256]{1,0:T(8,128)(2,1)}, u32[]{:S(2)}) copy-start(bf16[768,256]{1,0:T(8,128)(2,1)} %constant.18.clone.fl_ref) | copy-start | bytes 1179652
  23.3 3.7 %copy-start.3 = (bf16[768,256]{1,0:T(8,128)(2,1)S(1)}, bf16[768,256]{1,0:T(8,128)(2,1)}, u32[]{:S(2)}) copy-start(bf16[768,256]{1,0:T(8,128)(2,1)} %constant.20.clone.bl_ref) | copy-start | bytes 1179652
  23.3 3.7 %copy-start.4 = (f32[2,128,128]{2,1,0:T(8,128)S(1)}, f32[2,128,128]{2,1,0:T(8,128)}, u32[]{:S(2)}) copy-start(f32[2,128,128]{2,1,0:T(8,128)} %constant.21.clone.tw_ref) | copy-start | bytes 393220

commit v2 on v1

--- a/solution.py
+++ b/solution.py
@@ -3,7 +3,6 @@
 
 import jax
 import jax.numpy as jnp
-import ml_dtypes
 import numpy as np
 from jax import lax
 from jax.experimental import pallas as pl
@@ -24,22 +23,12 @@
 BF16 = jnp.bfloat16
 
 
-def split_np(matrix):
-    high = matrix.astype(ml_dtypes.bfloat16)
-    low = (matrix - high.astype(np.float64)).astype(ml_dtypes.bfloat16)
-    return high, low
-
-
 def left_form(matrix):
-    real = np.block([[matrix.real, -matrix.imag], [matrix.imag, matrix.real]])
-    high, low = split_np(real)
-    return np.concatenate([high, low, high], axis=1)
+    return np.block([[matrix.real, -matrix.imag], [matrix.imag, matrix.real]])
 
 
 def right_form(matrix):
-    real = np.block([[matrix.real, matrix.imag], [-matrix.imag, matrix.real]])
-    high, low = split_np(real)
-    return np.concatenate([high, high, low], axis=0)
+    return np.block([[matrix.real, matrix.imag], [-matrix.imag, matrix.real]])
 
 
 def dft_constants():
@@ -54,13 +43,27 @@
     rows = [turn(y1 * r / 8 + x0 * p / 16 + x0 * h / 32) for h in range(2)]
     lanes = turn(y0 * s / 4 + z * qz / 32)
     twist = turn(r * y0.T / 32)
+    steps = [left_form(m) for m in rows] + [left_form(m.conj().T) for m in rows]
+    steps += [right_form(lanes), right_form(lanes.conj().T)]
     return (
-        np.stack([left_form(m) for m in rows]),
-        right_form(lanes),
-        np.stack([left_form(m.conj().T) for m in rows]),
-        right_form(lanes.conj().T),
+        np.stack(steps).astype(np.float32),
         np.stack([twist.real, twist.imag]).astype(np.float32),
+        mirrors().astype(np.float32),
     )
+
+
+def mirrors():
+    lane = np.arange(LANES)
+    s, qz = lane // NV, lane % NV
+    moves = []
+    for carry in range(2):
+        source = (-s - carry) % 4 * NV + -qz % NV
+        moves.append((lane[:, None] == source[None, :]).astype(np.float64))
+    row = np.arange(NV * SUB)
+    h, r, p = row // LANES, row // 16 % 8, row % 16
+    source = h * LANES + -r % 8 * 16 + (-p - h) % 16
+    rows = (source[:, None] == row[None, :]).astype(np.float64)
+    return np.concatenate([np.concatenate(moves, axis=1), rows])
 
 
 def halves(value):
@@ -80,11 +83,14 @@
 
 def kernel(
     n_space, n_vel, cells, width,
-    dist_ref, listed_ref, weight_ref, fr_ref, fl_ref, br_ref, bl_ref, tw_ref,
-    out_ref,
-    padded, halo_out, halo_in, sent, got, result, back, spectrum, parts,
-    in_sem, halo_send, halo_recv, fs_sem, fr_sem, bs_sem, br_sem, own_sem,
+    dist_ref, order_ref, blocks_ref, kernels_ref, *refs,
 ):
+    tables_hbm, out_ref, refs = refs[:3], refs[3], refs[4:]
+    tables, refs = refs[:3], refs[3:]
+    step_ref, tw_ref, mirror_ref = tables
+    (padded, halo_out, halo_in, sent, got, result, back, spectrum, parts,
+    left_ref, right_ref, raw, natural, weight_ref, staged, listed_ref, raw_sem, in_sem, table_sem, out_sem,
+    halo_send, halo_recv, fs_sem, fr_sem, bs_sem, br_sem, own_sem) = refs
     rows = width // LANES
     own = cells // n_vel
     groups = own // GROUP
@@ -96,6 +102,14 @@
 
     load = pltpu.make_async_copy(dist_ref, padded.at[pl.ds(SUB, cells)], in_sem)
     load.start()
+    load_raw = pltpu.make_async_copy(kernels_ref, raw, raw_sem)
+    load_raw.start()
+    load_tables = [
+        pltpu.make_async_copy(source, table, table_sem.at[i])
+        for i, (source, table) in enumerate(zip(tables_hbm, tables))
+    ]
+    for copy in load_tables:
+        copy.start()
     barrier = pltpu.get_barrier_semaphore()
     for step in range(1, n_vel):
         pl.semaphore_signal(
@@ -124,30 +138,27 @@
         )
         copy.start()
         halo_copies.append(copy)
-    for copy in halo_copies:
-        copy.wait()
-
-    total = cells + 2 * SUB
-    position = lax.broadcasted_iota(jnp.int32, (total, LANES), 0) + (spot * cells - SUB)
-    inside = (position >= 0) & (position < n_space * cells)
+
+    def swept(value, k, inside=None):
+        plane = (me * rows + k) // SUB
+        courant = COURANT_MAX * (2.0 * plane.astype(F32) - (NV - 1)) / (NV - 1)
+        upwind_pos, upwind_neg = jnp.maximum(courant, 0.0), jnp.minimum(courant, 0.0)
+        extent = value.shape[0]
+        for _ in range(2):
+            before = pltpu.roll(value, 1, 0)
+            after = pltpu.roll(value, extent - 1, 0)
+            value = value - upwind_pos * (value - before) - upwind_neg * (after - value)
+            if inside is not None:
+                value = jnp.where(inside, value, 0.0)
+        return value
 
     @pl.loop(0, rows)
     def _(k):
         lanes = pl.ds(pl.multiple_of(k * LANES, LANES), LANES)
-        padded[SUB - 2:SUB, lanes] = halo_in[0, pl.ds(2 * k, 2), :]
-        padded[SUB + cells:SUB + cells + 2, lanes] = halo_in[1, pl.ds(2 * k, 2), :]
-        plane = (me * rows + k) // SUB
-        courant = COURANT_MAX * (2.0 * plane.astype(F32) - (NV - 1)) / (NV - 1)
-        upwind_pos, upwind_neg = jnp.maximum(courant, 0.0), jnp.minimum(courant, 0.0)
-        value = jnp.where(inside, padded[:, lanes], 0.0)
-        for _ in range(2):
-            before = pltpu.roll(value, 1, 0)
-            after = pltpu.roll(value, total - 1, 0)
-            value = value - upwind_pos * (value - before) - upwind_neg * (after - value)
-            value = jnp.where(inside, value, 0.0)
+        value = swept(padded[SUB:SUB + cells, lanes], k)
         for tile in range(cells // SUB):
             sent[pl.ds(tile * SUB * rows + k, SUB, stride=rows), :] = value[
-                (tile + 1) * SUB:(tile + 2) * SUB
+                tile * SUB:(tile + 1) * SUB
             ]
 
     def forward(group, step):
@@ -184,19 +195,95 @@
             own_sem.at[1, group],
         )
 
-    for group in range(groups):
+    def send(group):
         for step in range(1, n_vel):
             forward(group, step).start()
         own_in(group).start()
 
+    inner = [group for group in range(groups) if 0 < group < groups - 1]
+    outer = [group for group in range(groups) if group not in inner]
+    for group in inner:
+        send(group)
+    for copy in halo_copies:
+        copy.wait()
+
+    edge = 2 * SUB
+    for side in range(2):
+        base = 0 if side == 0 else cells
+        position = lax.broadcasted_iota(jnp.int32, (edge, LANES), 0) + (spot * cells + base - SUB)
+        inside = (position >= 0) & (position < n_space * cells)
+
+        @pl.loop(0, rows)
+        def _(k):
+            lanes = pl.ds(pl.multiple_of(k * LANES, LANES), LANES)
+            if side == 0:
+                padded[SUB - 2:SUB, lanes] = halo_in[0, pl.ds(2 * k, 2), :]
+            else:
+                padded[SUB + cells:SUB + cells + 2, lanes] = halo_in[1, pl.ds(2 * k, 2), :]
+            value = jnp.where(inside, padded[base:base + edge, lanes], 0.0)
+            value = swept(value, k, inside)
+            if side == 0:
+                sent[pl.ds(k, 2, stride=rows), :] = value[SUB:SUB + 2]
+            else:
+                sent[pl.ds((cells - 2) * rows + k, 2, stride=rows), :] = value[SUB - 2:SUB]
+
+    for group in outer:
+        send(group)
+
+    slot = lax.broadcasted_iota(jnp.int32, (cells, cells), 1)
+    cell_id = lax.broadcasted_iota(jnp.int32, (cells, cells), 0)
+    chosen = slot < BLOCK_CELLS * jnp.broadcast_to(blocks_ref[...], (cells, cells))
+    hit = (jnp.broadcast_to(order_ref[...], (cells, cells)) == cell_id) & chosen
+    flags = jnp.max(jnp.where(hit, 1.0, 0.0), axis=1, keepdims=True)
+    listed_ref[...] = jnp.broadcast_to(flags, (cells, LANES))
+
+    load_raw.wait()
+    for copy in load_tables:
+        copy.wait()
+    for i in range(4):
+        high, low = halves(step_ref[i])
+        left_ref[i] = jnp.concatenate([high, low, high], axis=1)
+    for i in range(2):
+        high, low = halves(step_ref[4 + i])
+        right_ref[i] = jnp.concatenate([high, high, low], axis=0)
+    for k in range(NV * SUB):
+        natural[pl.ds(k, KERN, stride=NV * SUB), :] = raw[:, k * LANES:(k + 1) * LANES]
+    lane_block = lax.broadcasted_iota(jnp.int32, (SUB, LANES), 1) // NV
+    row_r = lax.broadcasted_iota(jnp.int32, (NV * SUB, LANES), 0) // 16 % 8
+
+    @pl.loop(0, KERN)
+    def _(table):
+        base = table * (NV * SUB)
+        for h in range(2):
+            for r in range(8):
+                for p in (0, 8):
+                    packed = None
+                    for s in range(4):
+                        start = (2 * p + h) * SUB + 2 * s + r // 4
+                        block = natural[pl.ds(base + start, SUB, stride=2 * SUB), :]
+                        shift = (s - r % 4) % 4 * NV
+                        if shift:
+                            block = pltpu.roll(block, shift, 1)
+                        packed = block if s == 0 else jnp.where(lane_block == s, block, packed)
+                    top = h * LANES + r * 16 + p
+                    staged[top:top + SUB, :] = packed
+        value = staged[...]
+        high, low = halves(value)
+        lane_moves, row_moves = mirror_ref[:LANES].astype(BF16), mirror_ref[LANES:].astype(BF16)
+        moved = jnp.dot(high, lane_moves, preferred_element_type=F32) + jnp.dot(
+            low, lane_moves, preferred_element_type=F32
+        )
+        moved = jnp.where(row_r == 0, moved[:, :LANES], moved[:, LANES:])
+        high, low = halves(moved)
+        moved = jnp.dot(
+            row_moves, jnp.concatenate([high, low], axis=1), preferred_element_type=F32
+        )
+        moved = moved[:, :LANES] + moved[:, LANES:]
+        weight_ref[table] = (value + moved) * (0.5 / NV**3)
+
     half = NV * SUB // 2
 
-    @pl.loop(0, groups)
-    def _(group):
-        for step in range(1, n_vel):
-            forward(group, step).wait_recv()
-        own_in(group).wait()
-
+    def work(group):
         def cell(j):
             return jnp.concatenate(
                 [got[group, m, j * rows:(j + 1) * rows, :] for m in range(n_vel)], axis=0
@@ -215,20 +302,20 @@
         twist_re, twist_im = tw_ref[0], tw_ref[1]
         low, high = stacked(True), stacked(False)
         for h, mixed in enumerate((low + high, low - high)):
-            turned = left_dot(fr_ref[h], mixed)
+            turned = left_dot(left_ref[h], mixed)
             for i in range(pairs):
                 re = turned[:half, i * LANES:(i + 1) * LANES]
                 im = turned[half:, i * LANES:(i + 1) * LANES]
                 spectrum[(2 * i + h) * half:(2 * i + h + 1) * half, :] = jnp.concatenate(
                     [re * twist_re - im * twist_im, re * twist_im + im * twist_re], axis=1
                 )
-        spectrum[...] = right_dot(spectrum[...], fl_ref[...])
+        spectrum[...] = right_dot(spectrum[...], right_ref[0])
 
         for table in range(KERN):
             weight = weight_ref[table]
             weights = jnp.concatenate([weight] * pairs, axis=0)
             weights = jnp.concatenate([weights, weights], axis=1)
-            lined = right_dot(spectrum[...] * weights, bl_ref[...])
+            lined = right_dot(spectrum[...] * weights, right_ref[1])
             halves_out = []
             for h in range(2):
                 columns = []
@@ -240,7 +327,7 @@
                             [re * twist_re + im * twist_im, im * twist_re - re * twist_im], axis=0
                         )
                     )
-                halves_out.append(left_dot(br_ref[h], jnp.concatenate(columns, axis=1)))
+                halves_out.append(left_dot(left_ref[2 + h], jnp.concatenate(columns, axis=1)))
             even, odd = halves_out
             for place, value in ((0, even + odd), (1, even - odd)):
                 if table == 0:
@@ -268,31 +355,80 @@
                 result[group, m, j * rows:(j + 1) * rows, :] = jnp.where(
                     flag, old + STEP_SCALE * change, old
                 )
+
+    def give(group):
         for step in range(1, n_vel):
             backward(group, step).start()
         own_out(group).start()
 
+    turns = inner + outer
+    count = len(inner)
+
+    def group_of(turn):
+        if groups == 1:
+            return turn
+        return jnp.where(turn < count, turn + 1, (turn - count) * (groups - 1))
+
+    @pl.loop(0, groups)
+    def _(turn):
+        group = group_of(turn)
+        for step in range(1, n_vel):
+            forward(group, step).wait_recv()
+        own_in(group).wait()
+        if groups > 2:
+            @pl.when(turn == groups - 1)
+            def _():
+                give(group_of(turn - 1))
+
+        work(group)
+
+        if groups > 2:
+            @pl.when((turn > 0) & (turn < groups - 1))
+            def _():
+                give(group_of(turn - 1))
+
+            @pl.when(turn == groups - 1)
+            def _():
+                give(group)
+        else:
+            give(group)
+
     for group in range(groups):
         for step in range(1, n_vel):
             forward(group, step).wait_send()
+
+    def finish(tiles):
+        @pl.loop(0, rows)
+        def _(k):
+            lanes = pl.ds(pl.multiple_of(k * LANES, LANES), LANES)
+            for tile in tiles:
+                padded[tile * SUB:(tile + 1) * SUB, lanes] = back[
+                    pl.ds(tile * SUB * rows + k, SUB, stride=rows), :
+                ]
+
+        copies = []
+        for tile in tiles:
+            part = pl.ds(tile * SUB, SUB)
+            copies.append(pltpu.make_async_copy(padded.at[part], out_ref.at[part], out_sem.at[tile]))
+            copies[-1].start()
+        return copies
+
+    done, ready, copies = set(), set(), []
+    for group in turns:
+        for step in range(1, n_vel):
             backward(group, step).wait()
         own_out(group).wait()
-
-    @pl.loop(0, rows)
-    def _(k):
-        lanes = pl.ds(pl.multiple_of(k * LANES, LANES), LANES)
+        ready.add(group)
+        tiles = []
         for tile in range(cells // SUB):
-            out_ref[tile * SUB:(tile + 1) * SUB, lanes] = back[
-                pl.ds(tile * SUB * rows + k, SUB, stride=rows), :
-            ]
-
-
-def packed_weights(kernels):
-    cube = kernels.reshape(KERN, NV, NV, NV)
-    mirrored = jnp.roll(jnp.flip(cube, (1, 2, 3)), (1, 1, 1), (1, 2, 3))
-    even = (cube + mirrored) * (0.5 / NV**3)
-    even = even.reshape(KERN, NV // 2, 2, 4, 8, NV).transpose(0, 2, 4, 1, 3, 5)
-    return even.reshape(KERN, NV * SUB, LANES)
+            needs = {cell % own // GROUP for cell in range(tile * SUB, (tile + 1) * SUB)}
+            if tile not in done and needs <= ready:
+                tiles.append(tile)
+        done.update(tiles)
+        if tiles:
+            copies += finish(tiles)
+    for copy in copies:
+        copy.wait()
 
 
 def local(n_space, n_vel, distribution, collision_order, collision_blocks, kernels):
@@ -301,20 +437,17 @@
     own = cells // n_vel
     groups = own // GROUP
     piece = GROUP * rows
-    slot = lax.iota(jnp.int32, cells)
-    chosen = (slot < BLOCK_CELLS * collision_blocks[0])[:, None]
-    hit = (collision_order[0][:, None] == slot[None, :]) & chosen
-    listed = jnp.broadcast_to(jnp.max(hit.astype(F32), axis=0)[:, None], (cells, LANES))
-    weights = packed_weights(kernels)
     constants = [jnp.asarray(c) for c in dft_constants()]
+    anywhere = pl.BlockSpec(memory_space=pl.ANY)
     vmem = pl.BlockSpec(memory_space=pltpu.VMEM)
     dma = pltpu.SemaphoreType.DMA
     return pl.pallas_call(
         functools.partial(kernel, n_space, n_vel, cells, width),
         out_shape=jax.ShapeDtypeStruct((cells, width), F32),
-        in_specs=[pl.BlockSpec(memory_space=pl.ANY)] + [vmem] * 7,
-        out_specs=vmem,
-        scratch_shapes=[
+        in_specs=[anywhere, vmem, vmem] + [anywhere] * 4,
+        out_specs=anywhere,
+        scratch_shapes=[pltpu.VMEM(c.shape, c.dtype) for c in constants]
+        + [
             pltpu.VMEM((cells + 2 * SUB, width), F32),
             pltpu.VMEM((2, 2 * rows, LANES), F32),
             pltpu.VMEM((2, 2 * rows, LANES), F32),
@@ -324,7 +457,17 @@
             pltpu.VMEM((cells * rows, LANES), F32),
             pltpu.VMEM((GROUP // 2 * NV * SUB, 2 * LANES), F32),
             pltpu.VMEM((4, NV * SUB, GROUP // 2 * LANES), F32),
+            pltpu.VMEM((4, NV * SUB, 3 * NV * SUB), BF16),
+            pltpu.VMEM((2, 3 * NV * SUB, NV * SUB), BF16),
+            pltpu.VMEM((KERN, NV**3), F32),
+            pltpu.VMEM((KERN * NV * SUB, LANES), F32),
+            pltpu.VMEM((KERN, NV * SUB, LANES), F32),
+            pltpu.VMEM((NV * SUB, LANES), F32),
+            pltpu.VMEM((cells, LANES), F32),
             dma,
+            dma,
+            dma((len(constants),)),
+            dma((cells // SUB,)),
             dma((2,)),
             dma((2,)),
             dma((groups, n_vel)),
@@ -334,9 +477,9 @@
             dma((2, groups)),
         ],
         compiler_params=pltpu.CompilerParams(
-            collective_id=0, has_side_effects=True, vmem_limit_bytes=48 * 2**20
+            collective_id=0, has_side_effects=True, vmem_limit_bytes=60 * 2**20
         ),
-    )(distribution, listed, weights, *constants)
+    )(distribution, collision_order, collision_blocks[:, None], kernels, *constants)
 
 
 def solution(mesh):

time: 90.6 us -> 62 us (0.68)
  local copies, waits for them, and re-layouts: 21.6 us -> 3.06 us
  other arithmetic: 5.98 us -> 0 us
  Pallas kernels: 61.9 us -> 58.2 us
    slice x5 -> x0, local copies, waits for them, and re-layouts: 9.49 us -> none  [packed_weights(): mirrored = jnp.roll(jnp.flip(cube, (1, 2, 3)), (1, 1, 1), (1, 2, 3))]
    reshape x3 -> x0, local copies, waits for them, and re-layouts: 8.4 us -> none  [the longest x2 5.62 us: packed_weights(): cube = kernels.reshape(KERN, NV, NV, NV)]
    pallas_call x1, Pallas kernels: 61.9 us -> 58.2 us  [local(): pl.pallas_call(functools.partial(kernel, n_space, n_vel, cells, width), o...]
    transpose x1 -> x0, other arithmetic: 3.44 us -> none  [packed_weights(): even = even.reshape(KERN, NV // 2, 2, 4, 8, NV).transpose(0, 2, 4, 1, 3, 5)]
    concatenate x1 -> x0, other arithmetic: 2.44 us -> none  [packed_weights(): mirrored = jnp.roll(jnp.flip(cube, (1, 2, 3)), (1, 1, 1), (1, 2, 3))]
    transpose x1 -> x0, local copies, waits for them, and re-layouts: 2.24 us -> none  [packed_weights(): even = even.reshape(KERN, NV // 2, 2, 4, 8, NV).transpose(0, 2, 4, 1, 3, 5)]
    unnamed x13 -> x1, local copies, waits for them, and re-layouts: 1.35 us -> 3.06 us
where the time goes in v2:
time: 62 us; the launch traced here: 61.9 us
  Pallas kernels  58.2 us (94%)
  local copies, waits for them, and re-layouts  3.06 us (5%)
  between operations  0.66 us (1%)
    pallas_call x1, Pallas kernels, local(): pl.pallas_call(functools.partial(kernel, n_space, n_vel, cells, width), o...  58.2 us
    unnamed x1, local copies, waits for them, and re-layouts  3.06 us

profile of v2, /device:TPU:0, one launch (start us, length us, event | category | flops | bytes accessed | tf_op | source)
XLA Modules:
  0.0 61.9 jit_solution(3624826399932812777)
XLA Ops:
  0.7 58.2 %shard_map.73 = f32[64,8192]{1,0:T(8,128)} custom-call(f32[64,8192]{1,0:T(8,128)} %dist_ref.1, s32[1,64]{1,0:T(1,128)} %order_ref.1, s32[1,1]{1,0:T(1,128)} %bitcast.1.blocks_ref, f32[5,32768]{1,0:T(8,128)} %kernels_ref.1, f32[6,256,256]{2,1,0:T(8,128)} %constant.6.clone.refs_0_, f32[2,128,128]{2,1,0:T(8,128)} %constant.7.clone.refs_1_, ...), custom_call_target="tpu_custom_call" | custom-call | tf_op jit(solution)/shard_map/pallas_call | solution.py:444
  58.8 3.1 %copy.10 = f32[64,8192]{1,0:T(8,128)} copy(f32[64,8192]{1,0:T(8,128)} %shard_map.73) | data formatting | bytes 4194304

commit v3 on v2

--- a/solution.py
+++ b/solution.py
@@ -89,7 +89,7 @@
     tables, refs = refs[:3], refs[3:]
     step_ref, tw_ref, mirror_ref = tables
     (padded, halo_out, halo_in, sent, got, result, back, spectrum, parts,
-    left_ref, right_ref, raw, natural, weight_ref, staged, listed_ref, raw_sem, in_sem, table_sem, out_sem,
+    left_ref, right_ref, raw, natural, weight_ref, staged, listed_ref, raw_sem, in_sem, table_sem,
     halo_send, halo_recv, fs_sem, fr_sem, bs_sem, br_sem, own_sem) = refs
     rows = width // LANES
     own = cells // n_vel
@@ -152,15 +152,6 @@
                 value = jnp.where(inside, value, 0.0)
         return value
 
-    @pl.loop(0, rows)
-    def _(k):
-        lanes = pl.ds(pl.multiple_of(k * LANES, LANES), LANES)
-        value = swept(padded[SUB:SUB + cells, lanes], k)
-        for tile in range(cells // SUB):
-            sent[pl.ds(tile * SUB * rows + k, SUB, stride=rows), :] = value[
-                tile * SUB:(tile + 1) * SUB
-            ]
-
     def forward(group, step):
         target = lax.rem(me + step, n_vel)
         return pltpu.make_async_remote_copy(
@@ -202,30 +193,44 @@
 
     inner = [group for group in range(groups) if 0 < group < groups - 1]
     outer = [group for group in range(groups) if group not in inner]
-    for group in inner:
-        send(group)
+    if inner:
+        for step in [*range(1, n_vel), 0]:
+            target = lax.rem(me + step, n_vel)
+            first = pl.multiple_of(target * own, SUB)
+
+            @pl.loop(0, rows)
+            def _(k):
+                lanes = pl.ds(pl.multiple_of(k * LANES, LANES), LANES)
+                value = swept(padded[pl.ds(SUB + first, own), lanes], k)
+                for tile in range(own // SUB):
+                    sent[pl.ds((first + tile * SUB) * rows + k, SUB, stride=rows), :] = value[
+                        tile * SUB:(tile + 1) * SUB
+                    ]
+
+            for group in inner:
+                if step:
+                    forward(group, step).start()
+                else:
+                    own_in(group).start()
     for copy in halo_copies:
         copy.wait()
 
-    edge = 2 * SUB
-    for side in range(2):
-        base = 0 if side == 0 else cells
-        position = lax.broadcasted_iota(jnp.int32, (edge, LANES), 0) + (spot * cells + base - SUB)
-        inside = (position >= 0) & (position < n_space * cells)
-
-        @pl.loop(0, rows)
-        def _(k):
-            lanes = pl.ds(pl.multiple_of(k * LANES, LANES), LANES)
-            if side == 0:
-                padded[SUB - 2:SUB, lanes] = halo_in[0, pl.ds(2 * k, 2), :]
-            else:
-                padded[SUB + cells:SUB + cells + 2, lanes] = halo_in[1, pl.ds(2 * k, 2), :]
-            value = jnp.where(inside, padded[base:base + edge, lanes], 0.0)
-            value = swept(value, k, inside)
-            if side == 0:
-                sent[pl.ds(k, 2, stride=rows), :] = value[SUB:SUB + 2]
-            else:
-                sent[pl.ds((cells - 2) * rows + k, 2, stride=rows), :] = value[SUB - 2:SUB]
+    total = cells + 2 * SUB
+    position = lax.broadcasted_iota(jnp.int32, (total, LANES), 0) + (spot * cells - SUB)
+    inside = (position >= 0) & (position < n_space * cells)
+
+    @pl.loop(0, rows)
+    def _(k):
+        lanes = pl.ds(pl.multiple_of(k * LANES, LANES), LANES)
+        padded[SUB - 2:SUB, lanes] = halo_in[0, pl.ds(2 * k, 2), :]
+        padded[SUB + cells:SUB + cells + 2, lanes] = halo_in[1, pl.ds(2 * k, 2), :]
+        value = swept(jnp.where(inside, padded[:, lanes], 0.0), k, inside)
+        for target in range(n_vel):
+            for group in outer:
+                cell = target * own + group * GROUP
+                sent[pl.ds(cell * rows + k, GROUP, stride=rows), :] = value[
+                    SUB + cell:SUB + cell + GROUP
+                ]
 
     for group in outer:
         send(group)
@@ -402,18 +407,11 @@
         def _(k):
             lanes = pl.ds(pl.multiple_of(k * LANES, LANES), LANES)
             for tile in tiles:
-                padded[tile * SUB:(tile + 1) * SUB, lanes] = back[
+                out_ref[tile * SUB:(tile + 1) * SUB, lanes] = back[
                     pl.ds(tile * SUB * rows + k, SUB, stride=rows), :
                 ]
 
-        copies = []
-        for tile in tiles:
-            part = pl.ds(tile * SUB, SUB)
-            copies.append(pltpu.make_async_copy(padded.at[part], out_ref.at[part], out_sem.at[tile]))
-            copies[-1].start()
-        return copies
-
-    done, ready, copies = set(), set(), []
+    done, ready = set(), set()
     for group in turns:
         for step in range(1, n_vel):
             backward(group, step).wait()
@@ -426,9 +424,7 @@
                 tiles.append(tile)
         done.update(tiles)
         if tiles:
-            copies += finish(tiles)
-    for copy in copies:
-        copy.wait()
+            finish(tiles)
 
 
 def local(n_space, n_vel, distribution, collision_order, collision_blocks, kernels):
@@ -445,7 +441,7 @@
         functools.partial(kernel, n_space, n_vel, cells, width),
         out_shape=jax.ShapeDtypeStruct((cells, width), F32),
         in_specs=[anywhere, vmem, vmem] + [anywhere] * 4,
-        out_specs=anywhere,
+        out_specs=vmem,
         scratch_shapes=[pltpu.VMEM(c.shape, c.dtype) for c in constants]
         + [
             pltpu.VMEM((cells + 2 * SUB, width), F32),
@@ -467,7 +463,6 @@
             dma,
             dma,
             dma((len(constants),)),
-            dma((cells // SUB,)),
             dma((2,)),
             dma((2,)),
             dma((groups, n_vel)),

time: 62 us -> 61.6 us (level)
  no operation moved by 1% of the time
where the time goes in v3:
time: 61.6 us; the launch traced here: 61.4 us
  Pallas kernels  57.7 us (94%)
  local copies, waits for them, and re-layouts  3.06 us (5%)
  between operations  0.66 us (1%)
    pallas_call x1, Pallas kernels, local(): pl.pallas_call(functools.partial(kernel, n_space, n_vel, cells, width), o...  57.7 us
    unnamed x1, local copies, waits for them, and re-layouts  3.06 us

profile of v3, /device:TPU:0, one launch (start us, length us, event | category | flops | bytes accessed | tf_op | source)
XLA Modules:
  0.0 61.4 jit_solution(12806264975982749376)
XLA Ops:
  0.7 57.7 %shard_map.73 = f32[64,8192]{1,0:T(8,128)} custom-call(f32[64,8192]{1,0:T(8,128)} %dist_ref.1, s32[1,64]{1,0:T(1,128)} %order_ref.1, s32[1,1]{1,0:T(1,128)} %bitcast.1.blocks_ref, f32[5,32768]{1,0:T(8,128)} %kernels_ref.1, f32[6,256,256]{2,1,0:T(8,128)} %constant.6.clone.refs_0_, f32[2,128,128]{2,1,0:T(8,128)} %constant.7.clone.refs_1_, ...), custom_call_target="tpu_custom_call" | custom-call | tf_op jit(solution)/shard_map/pallas_call | solution.py:440
  58.3 3.1 %copy.10 = f32[64,8192]{1,0:T(8,128)} copy(f32[64,8192]{1,0:T(8,128)} %shard_map.73) | data formatting | bytes 4194304

commit v4 on v3

--- a/solution.py
+++ b/solution.py
@@ -380,51 +380,25 @@
         for step in range(1, n_vel):
             forward(group, step).wait_recv()
         own_in(group).wait()
-        if groups > 2:
-            @pl.when(turn == groups - 1)
-            def _():
-                give(group_of(turn - 1))
-
         work(group)
-
-        if groups > 2:
-            @pl.when((turn > 0) & (turn < groups - 1))
-            def _():
-                give(group_of(turn - 1))
-
-            @pl.when(turn == groups - 1)
-            def _():
-                give(group)
-        else:
-            give(group)
+        give(group)
 
     for group in range(groups):
         for step in range(1, n_vel):
             forward(group, step).wait_send()
 
-    def finish(tiles):
-        @pl.loop(0, rows)
-        def _(k):
-            lanes = pl.ds(pl.multiple_of(k * LANES, LANES), LANES)
-            for tile in tiles:
-                out_ref[tile * SUB:(tile + 1) * SUB, lanes] = back[
-                    pl.ds(tile * SUB * rows + k, SUB, stride=rows), :
-                ]
-
-    done, ready = set(), set()
     for group in turns:
         for step in range(1, n_vel):
             backward(group, step).wait()
         own_out(group).wait()
-        ready.add(group)
-        tiles = []
-        for tile in range(cells // SUB):
-            needs = {cell % own // GROUP for cell in range(tile * SUB, (tile + 1) * SUB)}
-            if tile not in done and needs <= ready:
-                tiles.append(tile)
-        done.update(tiles)
-        if tiles:
-            finish(tiles)
+        for source in range(n_vel):
+            part = pl.ds((source * groups + group) * piece, piece)
+            out_ref[part, :] = back[part, :]
+
+
+def regrid(rows, in_ref, out_ref):
+    for k in range(rows):
+        out_ref[:, k * LANES:(k + 1) * LANES] = in_ref[pl.ds(k, SUB, stride=rows), :]
 
 
 def local(n_space, n_vel, distribution, collision_order, collision_blocks, kernels):
@@ -437,9 +411,9 @@
     anywhere = pl.BlockSpec(memory_space=pl.ANY)
     vmem = pl.BlockSpec(memory_space=pltpu.VMEM)
     dma = pltpu.SemaphoreType.DMA
-    return pl.pallas_call(
+    moved = pl.pallas_call(
         functools.partial(kernel, n_space, n_vel, cells, width),
-        out_shape=jax.ShapeDtypeStruct((cells, width), F32),
+        out_shape=jax.ShapeDtypeStruct((cells * rows, LANES), F32),
         in_specs=[anywhere, vmem, vmem] + [anywhere] * 4,
         out_specs=vmem,
         scratch_shapes=[pltpu.VMEM(c.shape, c.dtype) for c in constants]
@@ -475,6 +449,14 @@
             collective_id=0, has_side_effects=True, vmem_limit_bytes=60 * 2**20
         ),
     )(distribution, collision_order, collision_blocks[:, None], kernels, *constants)
+    return pl.pallas_call(
+        functools.partial(regrid, rows),
+        grid=(cells // SUB,),
+        out_shape=jax.ShapeDtypeStruct((cells, width), F32),
+        in_specs=[pl.BlockSpec((SUB * rows, LANES), lambda i: (i, 0))],
+        out_specs=pl.BlockSpec((SUB, width), lambda i: (i, 0)),
+        compiler_params=pltpu.CompilerParams(vmem_limit_bytes=60 * 2**20),
+    )(moved)
 
 
 def solution(mesh):

time: 61.6 us -> 63.4 us (1.029)
  Pallas kernels: 57.7 us -> 62.5 us
  local copies, waits for them, and re-layouts: 3.06 us -> 0 us
    pallas_call x0 -> x1, Pallas kernels: none -> 6.11 us  [local(): pl.pallas_call(functools.partial(regrid, rows), grid=(cells // SUB,), out...]
    unnamed x1 -> x0, local copies, waits for them, and re-layouts: 3.06 us -> none
    pallas_call x1, Pallas kernels: 57.7 us -> 56.4 us  [local(): pl.pallas_call(functools.partial(kernel, n_space, n_vel, cells, width), o...]
where the time goes in v4:
time: 63.4 us; the launch traced here: 63.2 us
  Pallas kernels  62.5 us (99%)
  between operations  0.66 us (1%)
    pallas_call x1, Pallas kernels, local(): pl.pallas_call(functools.partial(kernel, n_space, n_vel, cells, width), o...  56.4 us
    pallas_call x1, Pallas kernels, local(): pl.pallas_call(functools.partial(regrid, rows), grid=(cells // SUB,), out...  6.11 us

profile of v4, /device:TPU:0, one launch (start us, length us, event | category | flops | bytes accessed | tf_op | source)
XLA Modules:
  0.0 63.2 jit_solution(11177271831606051159)
XLA Ops:
  0.7 56.4 %shard_map.73.in_ref = f32[4096,128]{1,0:T(8,128)} custom-call(f32[64,8192]{1,0:T(8,128)} %dist_ref.1, s32[1,64]{1,0:T(1,128)} %order_ref.1, s32[1,1]{1,0:T(1,128)} %bitcast.1.blocks_ref, f32[5,32768]{1,0:T(8,128)} %kernels_ref.1, f32[6,256,256]{2,1,0:T(8,128)} %constant.6.clone.refs_0_, f32[2,128,128]{2,1,0:T(8,128)} %constant.7.clone.refs_1_, ...), custom_call_target="tpu_custom_call" | custom-call | tf_op jit(solution)/shard_map/pallas_call | solution.py:414
  57.1 6.1 %shard_map.74 = f32[64,8192]{1,0:T(8,128)} custom-call(f32[4096,128]{1,0:T(8,128)} %shard_map.73.in_ref), custom_call_target="tpu_custom_call" | custom-call | tf_op jit(solution)/shard_map/pallas_call | solution.py:452
